TPU v7x, 32 devices: a whole 2x2x4 slice. The times are simulated.
32 devices in a mesh: plane: 16 (over z, y, core), thick: 2 (over x).
Axes of the slice: x: 2, y: 2, z: 4, core: 2. Of those that a mesh axis runs over, the one named last changes fastest.
Arguments:
- solid: int32 [4, 16, 8, 128], P('thick', 'plane'), may hold values 0 or 1
- labels: int32 [4, 16, 8, 128], P('thick', 'plane'), may hold values 0 or 1
- density: float32 [4, 16, 8, 128], P('thick', 'plane'), may hold values from 0.5 to 2
- wettability: float32 [4, 16, 8, 128], P('thick', 'plane'), may hold values from -1 to 1
- direction: float32 [4, 16, 8, 128], P('thick', 'plane'), may hold values from -6 to 6
- pixel_map: int32 [16, 8, 128], P('plane'), may hold values from 0 to 127
Outputs:
- curvature: float32 [4, 16, 8, 128], P('thick', 'plane')
- readings: float32 [16, 8, 128], P('plane')
All inputs are finite; a program needn't handle non-finite values. No bound on the sum of `solid` or of `labels` on one device may be relied on, other than what follows from the above.
Results may differ from a plain program's by a relative error of at most 0.0001.
Values sent between devices are 32-bit elements; how exact they have to be, the bound alone decides.
No kernel may reach another device: no remote copies, remote signals or barrier semaphores. Data moves between devices by JAX's collectives and lax.ppermute only.
A program may use at most 64 MiB of HBM per device.

v0:
```python
import functools

import jax
import jax.numpy as jnp
import numpy as np
from jax import lax
from jax.experimental import pallas as pl
from jax.experimental.pallas import tpu as pltpu
from jax.sharding import PartitionSpec as P

NBX = 8
STEPS = 2


VELOCITIES = np.array(
    [
        [0, 0, 0],
        [1, 0, 0],
        [-1, 0, 0],
        [0, 1, 0],
        [0, -1, 0],
        [0, 0, 1],
        [0, 0, -1],
        [1, 1, 0],
        [-1, -1, 0],
        [1, -1, 0],
        [-1, 1, 0],
        [1, 0, 1],
        [-1, 0, -1],
        [1, 0, -1],
        [-1, 0, 1],
        [0, 1, 1],
        [0, -1, -1],
        [0, 1, -1],
        [0, -1, 1],
    ]
)
WEIGHTS = np.array([1.0 / 3.0] + [1.0 / 18.0] * 6 + [1.0 / 36.0] * 12)
OPPOSITE = [int(np.argmin(np.abs(VELOCITIES + lattice_vec).sum(1))) for lattice_vec in VELOCITIES]
RELAX_RATE = 1.25
SURFACE_TENSION = 0.2
RECOLOURING_PACE = 0.7


def shifted(array, axis, by):
    devices = lax.axis_size(axis)
    pairs = [(i, i + by) for i in range(devices) if 0 <= i + by < devices]
    return lax.ppermute(array, axis, pairs)


def from_behind(block, axis, distance):
    devices = range(lax.axis_size(axis))
    route = [((i - distance) % len(devices), i) for i in devices]
    return lax.ppermute(block, axis, route)


def weights_like(array):
    return jnp.asarray(WEIGHTS, jnp.float32).reshape((19,) + (1,) * (array.ndim - 1))


def collide(red_pop, blue_pop, gradient, solid_cell):
    lattice_vel = jnp.asarray(VELOCITIES, jnp.float32)
    weight_column_vec = weights_like(red_pop)
    red_density_total = jnp.sum(red_pop, 0)
    blue_density_total = jnp.sum(blue_pop, 0)
    density = red_density_total + blue_density_total
    reciprocal_value = 1.0 / (density + solid_cell)
    total_pop = red_pop + blue_pop
    velocity = (
        jnp.einsum("qd,q...->d...", lattice_vel, total_pop, precision=lax.Precision.HIGHEST)
        * reciprocal_value
    )
    projected = jnp.einsum("qd,d...->q...", lattice_vel, velocity, precision=lax.Precision.HIGHEST)
    speed_sq = jnp.sum(velocity * velocity, 0)
    equilibrium = (
        weight_column_vec
        * density
        * (1.0 + 3.0 * projected + 4.5 * projected * projected - 1.5 * speed_sq)
    )
    relaxed_populations = total_pop + RELAX_RATE * (equilibrium - total_pop)
    along_gradient_dir = jnp.einsum(
        "qd,d...->q...", lattice_vel, gradient, precision=lax.Precision.HIGHEST
    )
    grad_sq = jnp.sum(gradient * gradient, 0)
    norm_scale_factor = 1.0 / jnp.sqrt(1.0 + grad_sq)
    relaxed_populations = (
        relaxed_populations
        + SURFACE_TENSION
        * weight_column_vec
        * (along_gradient_dir * along_gradient_dir - grad_sq / 3.0)
        * norm_scale_factor
    )
    red_output_pop = (
        red_density_total * reciprocal_value * relaxed_populations
        + RECOLOURING_PACE
        * red_density_total
        * blue_density_total
        * reciprocal_value
        * weight_column_vec
        * along_gradient_dir
        * norm_scale_factor
    )
    return (red_output_pop, relaxed_populations - red_output_pop)


def phase_of(red_pop, blue_pop, solid_cell):
    red_density_total = jnp.sum(red_pop, 0)
    blue_density_total = jnp.sum(blue_pop, 0)
    return (red_density_total - blue_density_total) / (
        red_density_total + blue_density_total + solid_cell
    )


def pull_from(padded, offset, extent):
    shift_z, shift_x, shift_y = (int(offset[0]), int(offset[1]), int(offset[2]))
    return padded[
        ...,
        1 - shift_z : 1 - shift_z + extent[0],
        1 - shift_x : 1 - shift_x + extent[1],
        1 - shift_y : 1 - shift_y + extent[2],
    ]


def gradient_of(padded, extent):
    components = [0.0, 0.0, 0.0]
    for number in range(1, 19):
        lattice_vec = VELOCITIES[number]
        pulled = pull_from(padded, -lattice_vec, extent)
        for axis_num in range(3):
            if lattice_vec[axis_num] != 0:
                components[axis_num] = (
                    components[axis_num]
                    + 3.0 * WEIGHTS[number] * float(lattice_vec[axis_num]) * pulled
                )
    return jnp.stack(components)


def spread_back(padded_bar, extent):
    total_bar = 0.0
    for number in range(1, 19):
        lattice_vec = VELOCITIES[number]
        for axis_num in range(3):
            if lattice_vec[axis_num] != 0:
                total_bar = total_bar + 3.0 * WEIGHTS[number] * float(
                    lattice_vec[axis_num]
                ) * pull_from(padded_bar[axis_num], lattice_vec, extent)
    return total_bar


def stream(padded_pop, local_pop, padded_fluid, fluid_cell, extent):
    outgoing = []
    for number in range(19):
        lattice_vec = VELOCITIES[number]
        source_fluid = pull_from(padded_fluid, lattice_vec, extent)
        arrived = pull_from(padded_pop[number], lattice_vec, extent)
        outgoing.append(
            fluid_cell
            * (source_fluid * arrived + (1.0 - source_fluid) * local_pop[OPPOSITE[number]])
        )
    return jnp.stack(outgoing)


def unstream(padded_bar, local_bar, padded_fluid, fluid_cell, extent):
    incoming = []
    for number in range(19):
        lattice_vec = VELOCITIES[number]
        ahead_fluid = pull_from(padded_fluid, -lattice_vec, extent)
        ahead_bar = pull_from(padded_bar[number], -lattice_vec, extent)
        incoming.append(fluid_cell * ahead_bar + (1.0 - ahead_fluid) * local_bar[OPPOSITE[number]])
    return jnp.stack(incoming)


def fill_border(received, chosen, channels):
    if len(chosen) == channels:
        return received
    return (
        jnp.zeros((channels,) + received.shape[1:], received.dtype)
        .at[np.array(chosen)]
        .set(received)
    )


def grow(stacked, axis_dim, chosen_low, chosen_high, sender):
    length = stacked.shape[axis_dim]
    channels = stacked.shape[0]
    borders = []
    for toward in (1, -1):
        chosen = chosen_low if toward == 1 else chosen_high
        source = length - 1 if toward == 1 else 0
        outer_layer = lax.slice_in_dim(stacked, source, source + 1, axis=axis_dim)
        if len(chosen) < channels:
            outer_layer = outer_layer[np.array(chosen)]
        borders.append(fill_border(sender(outer_layer, toward), chosen, channels))
    return jnp.concatenate([borders[0], stacked, borders[1]], axis_dim)


def per_device(solid, labels, density, wettability, direction, pixel_map):
    solid_cell = solid[:, 0].astype(jnp.float32)
    fluid_cell = 1.0 - solid_cell
    label_cell = labels[:, 0].astype(jnp.float32)
    density_cell = density[:, 0]
    wetting = wettability[:, 0]
    tangent = direction[:, 0]
    column_map = pixel_map[0]
    extent = solid_cell.shape
    bricks_y = lax.axis_size("plane") // NBX

    def extend(stacked):
        channels = stacked.shape[0]

        def chosen_for():
            return list(range(channels))

        stacked = grow(
            stacked,
            1,
            chosen_for(),
            chosen_for(),
            lambda outgoing, toward: shifted(outgoing, "thick", toward),
        )
        stacked = grow(
            stacked,
            2,
            chosen_for(),
            chosen_for(),
            lambda outgoing, toward: from_behind(outgoing, "plane", toward * bricks_y),
        )
        stacked = grow(
            stacked,
            3,
            chosen_for(),
            chosen_for(),
            lambda outgoing, toward: from_behind(outgoing, "plane", toward),
        )
        return stacked

    def phase_pair(red_in, blue_in):
        return phase_of(red_in, blue_in, solid_cell)

    def collide_local(red_in, blue_in, gradient):
        return collide(red_in, blue_in, gradient, solid_cell)

    padded_fluid = extend(fluid_cell[None])[0]
    weight_column_vec = weights_like(solid_cell[None])
    red_pop = weight_column_vec * (density_cell * label_cell * fluid_cell)[None]
    blue_pop = weight_column_vec * (density_cell * (1.0 - label_cell) * fluid_cell)[None]
    red_tan = jnp.zeros_like(red_pop)
    blue_tan = jnp.zeros_like(blue_pop)
    checkpoints = []
    for number in range(STEPS):
        phase_val, phase_tan = jax.jvp(phase_pair, (red_pop, blue_pop), (red_tan, blue_tan))
        phase_field = fluid_cell * phase_val + solid_cell * wetting
        field_tan = fluid_cell * phase_tan + solid_cell * tangent
        padded = extend(jnp.stack([phase_field, field_tan]))
        gradient = gradient_of(padded[0], extent)
        gradient_tan = gradient_of(padded[1], extent)
        checkpoints.append((red_pop, blue_pop, gradient))
        (red_post, blue_post), (red_dot, blue_dot) = jax.jvp(
            collide_local, (red_pop, blue_pop, gradient), (red_tan, blue_tan, gradient_tan)
        )
        posted = jnp.concatenate([red_post, blue_post, red_dot, blue_dot])
        moved = extend(posted)
        red_pop, blue_pop, red_tan, blue_tan = [
            stream(
                moved[19 * group : 19 * group + 19],
                posted[19 * group : 19 * group + 19],
                padded_fluid,
                fluid_cell,
                extent,
            )
            for group in range(4)
        ]
    _, phase_tan = jax.jvp(phase_pair, (red_pop, blue_pop), (red_tan, blue_tan))
    partial_sum = jnp.sum(fluid_cell * phase_tan, 0)
    column_sum = lax.psum(partial_sum, "thick")
    found = jnp.take_along_axis(column_sum, column_map, axis=1)
    row_ids = jnp.arange(column_map.shape[0])[:, None]
    seeded = jnp.zeros_like(column_sum).at[row_ids, column_map].add(found)
    _, phase_back = jax.vjp(phase_pair, red_pop, blue_pop)
    red_bar, blue_bar = phase_back(fluid_cell * seeded[None])
    wetting_bar = jnp.zeros_like(wetting)
    for number in reversed(range(STEPS)):
        red_saved, blue_saved, gradient = checkpoints[number]
        outgoing_bar = jnp.concatenate([red_bar, blue_bar]) * fluid_cell
        padded = extend(outgoing_bar)
        red_pre = unstream(padded[:19], outgoing_bar[:19], padded_fluid, fluid_cell, extent)
        blue_pre = unstream(padded[19:], outgoing_bar[19:], padded_fluid, fluid_cell, extent)
        _, collide_back = jax.vjp(collide_local, red_saved, blue_saved, gradient)
        red_bar, blue_bar, gradient_bar = collide_back((red_pre, blue_pre))
        padded_bar = extend(gradient_bar)
        field_bar = spread_back(padded_bar, extent)
        wetting_bar = wetting_bar + solid_cell * field_bar
        if number > 0:
            _, phase_back = jax.vjp(phase_pair, red_saved, blue_saved)
            extra_red, extra_blue = phase_back(fluid_cell * field_bar)
            red_bar = red_bar + extra_red
            blue_bar = blue_bar + extra_blue
    return (wetting_bar[:, None], found[None])


HALF = 128
WIDE = 256
ROW_TILES = 3
Z_AXIS, X_AXIS, Y_AXIS = range(3)
EDGES = [(0, 1, 1), (0, 1, -1), (0, 2, 1), (0, 2, -1), (1, 2, 1), (1, 2, -1)]
CZ = [int(v[0]) for v in VELOCITIES]
CX = [int(v[1]) for v in VELOCITIES]
CY = [int(v[2]) for v in VELOCITIES]
GROUPS = [(gx, gy) for gx in (-1, 0, 1) for gy in (-1, 0, 1)]


def roll_rows(tile, by):
    return pltpu.roll(tile, by % tile.shape[0], 0)


def roll_lanes(tile, by):
    return pltpu.roll(tile, by % tile.shape[1], 1)


def x_shift(tiles, dx):
    row = lax.broadcasted_iota(jnp.int32, tiles[0].shape, 0)
    out = []
    for r in range(ROW_TILES):
        beyond = tiles[(r + dx) % ROW_TILES]
        edge = 0 if dx == 1 else 7
        out.append(roll_rows(jnp.where(row == edge, beyond, tiles[r]), -dx))
    return out


def y_shift(tiles, dy):
    return [roll_lanes(tile, -dy) for tile in tiles]


def each(function, *lists):
    return [function(*items) for items in zip(*lists)]


def add(a, b):
    return a + b


def sub(a, b):
    return a - b


def both_ways(shift, tiles):
    return shift(tiles, 1), shift(tiles, -1)


def plane(ref, zi):
    return [ref[zi, r] for r in range(ROW_TILES)]


def gradient_tiles(ref, zi):
    mid, up, down = plane(ref, zi), plane(ref, zi + 1), plane(ref, zi - 1)
    two = each(lambda m, u, d: 2.0 * m + u + d, mid, up, down)
    slope = each(sub, up, down)
    y_sum = each(add, *both_ways(y_shift, mid))
    x_sum = each(add, *both_ways(x_shift, mid))
    along_x = each(sub, *both_ways(x_shift, each(add, two, y_sum)))
    along_y = each(sub, *both_ways(y_shift, each(add, two, x_sum)))
    sx = each(add, *both_ways(x_shift, slope))
    sy = each(add, *both_ways(y_shift, slope))
    along_z = each(lambda s, a, b: 2.0 * s + a + b, slope, sx, sy)
    return along_z, along_x, along_y


def gradient_back(refs, zi):
    gz, gx, gy = refs
    mid, up, down = plane(gx, zi), plane(gx, zi + 1), plane(gx, zi - 1)
    y_sum = each(add, *both_ways(y_shift, mid))
    total = each(lambda m, u, d, s: 2.0 * m + u + d + s, mid, up, down, y_sum)
    result = each(sub, *both_ways(x_shift, total))
    mid, up, down = plane(gy, zi), plane(gy, zi + 1), plane(gy, zi - 1)
    x_sum = each(add, *both_ways(x_shift, mid))
    total = each(lambda m, u, d, s: 2.0 * m + u + d + s, mid, up, down, x_sum)
    result = each(add, result, each(sub, *both_ways(y_shift, total)))
    slope = each(sub, plane(gz, zi + 1), plane(gz, zi - 1))
    sx = each(add, *both_ways(x_shift, slope))
    sy = each(add, *both_ways(y_shift, slope))
    return each(lambda a, s, b, c: a + 2.0 * s + b + c, result, slope, sx, sy)


def even_part(base, quad):
    zz, xx, yy, zx, zy, xy = quad
    out = [2.0 * (base + zz), 2.0 * (base + xx), 2.0 * (base + yy)]
    for diagonal, cross in ((zz + xx, zx), (zz + yy, zy), (xx + yy, xy)):
        flat = base + diagonal
        out += [flat + cross, flat - cross]
    return out


def odd_part(vector):
    z, x, y = vector
    return [2.0 * z, 2.0 * x, 2.0 * y, z + x, z - x, z + y, z - y, x + y, x - y]


def squares(vector):
    z, x, y = vector
    return [z * z, x * x, y * y, 2.0 * (z * x), 2.0 * (z * y), 2.0 * (x * y)]


def squares_dot(a, b):
    az, ax, ay = a
    bz, bx, by = b
    return [
        2.0 * (az * bz),
        2.0 * (ax * bx),
        2.0 * (ay * by),
        2.0 * (az * bx + ax * bz),
        2.0 * (az * by + ay * bz),
        2.0 * (ax * by + ay * bx),
    ]


def dot(a, b):
    return a[0] * b[0] + a[1] * b[1] + a[2] * b[2]


def first_moment(values):
    d = [values[2 * p + 1] - values[2 * p + 2] for p in range(9)]
    return (
        d[0] + (d[3] + d[4]) + (d[5] + d[6]),
        d[1] + (d[3] - d[4]) + (d[7] + d[8]),
        d[2] + (d[5] - d[6]) + (d[7] - d[8]),
    )


def weighted_first(values):
    d = [values[2 * p + 1] - values[2 * p + 2] for p in range(9)]
    return (
        2.0 * d[0] + (d[3] + d[4]) + (d[5] + d[6]),
        2.0 * d[1] + (d[3] - d[4]) + (d[7] + d[8]),
        2.0 * d[2] + (d[5] - d[6]) + (d[7] - d[8]),
    )


def weighted_even(rest, pairs):
    axis = [2.0 * pairs[0], 2.0 * pairs[1], 2.0 * pairs[2]]
    zx, zy, xy = pairs[3] + pairs[4], pairs[5] + pairs[6], pairs[7] + pairs[8]
    second = [
        axis[0] + zx + zy,
        axis[1] + zx + xy,
        axis[2] + zy + xy,
        pairs[3] - pairs[4],
        pairs[5] - pairs[6],
        pairs[7] - pairs[8],
    ]
    zeroth = 12.0 * rest + axis[0] + axis[1] + axis[2] + zx + zy + xy
    return zeroth, second


def pair_sums(values):
    return [values[2 * p + 1] + values[2 * p + 2] for p in range(9)]


def times(matrix, vector):
    zz, xx, yy, zx, zy, xy = matrix
    z, x, y = vector
    return (zz * z + zx * x + zy * y, zx * z + xx * x + xy * y, zy * z + xy * x + yy * y)


def total(values):
    values = list(values)
    while len(values) > 1:
        values = [
            values[k] + values[k + 1] if k + 1 < len(values) else values[k]
            for k in range(0, len(values), 2)
        ]
    return values[0]


def norm_parts(g):
    g2 = dot(g, g)
    n = lax.rsqrt(1.0 + g2)
    return g2, n


def scatter_groups(acc, zi, r, values, stay):
    for k, (gx, gy) in enumerate(GROUPS):
        here = [i for i in range(1, 19) if (CX[i], CY[i]) == (gx, gy)]
        level = {CZ[i]: values[i] for i in here}
        if (gx, gy) == (0, 0):
            level[0] = values[0] + stay
        if 1 not in level:
            acc[k, zi, r] = level[0]
            continue
        acc[k, zi + 1, r] = level[1]
        acc[k, zi, r] = acc[k, zi, r] + level[0]
        acc[k, zi - 1, r] = acc[k, zi - 1, r] + level[-1]


def gathered_sum(acc, zi):
    by_y = []
    for gy in (-1, 0, 1):
        parts = [plane(acc.at[GROUPS.index((0, gy))], zi)]
        for gx in (-1, 1):
            parts.append(x_shift(plane(acc.at[GROUPS.index((gx, gy))], zi), -gx))
        by_y.append(each(lambda *a: total(a), *parts))
    return each(
        lambda a, b, c: a + b + c, y_shift(by_y[0], 1), by_y[1], y_shift(by_y[2], -1)
    )


def moved(ref, zi, i, sign):
    tiles = plane(ref, zi + sign * CZ[i])
    if CX[i]:
        tiles = x_shift(tiles, sign * CX[i])
    if CY[i]:
        tiles = y_shift(tiles, sign * CY[i])
    return tiles


def all_moved(ref, zi):
    out = [None] * 19
    for cz in (-1, 0, 1):
        base = plane(ref, zi + cz)
        rows = {0: base, 1: x_shift(base, 1), -1: x_shift(base, -1)}
        for i in range(19):
            if CZ[i] == cz:
                tiles = rows[CX[i]]
                out[i] = y_shift(tiles, CY[i]) if CY[i] else tiles
    return out


def main_kernel(nz, local_z, q_ref, qm_ref, qp_ref, sl_ref, map_ref, out_ref, read_ref,
                rho, p1, dp1, cnt, blk, t_st, dt_st, acc, pop, dpop, mac, p2, dp2, g1, g2s,
                a3, b3, col, adj, gbar, pbar2):
    thick = lax.axis_index("thick")
    even = lax.rem(lax.axis_index("plane"), 2) == 0
    per = 3 * local_z + 1
    f32 = jnp.float32
    zero_tile = jnp.zeros((8, WIDE), f32)

    for ref in (rho, p1, dp1, p2, dp2):
        for r in range(ROW_TILES):
            ref[0, r] = zero_tile
            ref[nz + 1, r] = zero_tile
    for k in range(3):
        for r in range(ROW_TILES):
            gbar[k, 0, r] = zero_tile
            gbar[k, nz + 1, r] = zero_tile
    for k in range(36):
        for r in range(ROW_TILES):
            acc[k, 1, r] = zero_tile
    lane = lax.broadcasted_iota(jnp.int32, (8, HALF), 1)
    low = lane < HALF // 2

    def sides(r, k, ks):
        if r == 0:
            middle = q_ref[2 * per + k]
            right = jnp.where(even, q_ref[k], qp_ref[k])
            left = jnp.where(even, qm_ref[k], q_ref[k])
        elif r == 1:
            middle = qp_ref[2 * per + k]
            right = jnp.where(even, qp_ref[k], sl_ref[ks])
            left = jnp.where(even, q_ref[k], qp_ref[k])
        else:
            middle = qm_ref[2 * per + k]
            right = jnp.where(even, qm_ref[k], q_ref[k])
            left = jnp.where(even, sl_ref[ks], qm_ref[k])
        return middle, jnp.where(low, right, left)

    for part in range(2):
        slab = thick if part == 0 else 1 - thick
        for zl in range(local_z):
            zi = 1 + slab * local_z + zl
            for r in range(ROW_TILES):
                for which, ref in enumerate((rho, p1, dp1)):
                    k = which * local_z + zl + part * per
                    middle, side = sides(r, k, k)
                    ref[zi, r, :, :HALF] = middle
                    ref[zi, r, :, HALF:] = side
    for r in range(ROW_TILES):
        middle, side = sides(r, per - 1, per - 1)
        cnt[r, :, :HALF] = middle
        cnt[r, :, HALF:] = side

    def links(z, carry):
        zi = z + 1
        here = each(lambda v: jnp.where(v == 0.0, 1.0, 0.0), plane(rho, zi))
        for cz in (-1, 0, 1):
            base = each(lambda v: jnp.where(v == 0.0, 1.0, 0.0), plane(rho, zi + cz))
            rows = {0: base, 1: x_shift(base, 1), -1: x_shift(base, -1)}
            for i in range(1, 19):
                if CZ[i] == cz:
                    tiles = rows[CX[i]]
                    tiles = y_shift(tiles, CY[i]) if CY[i] else tiles
                    for r in range(ROW_TILES):
                        blk[i - 1, z, r] = jnp.maximum(tiles[r], here[r])
        return carry

    lax.fori_loop(0, nz, links, 0)

    def link(z, r):
        return [None] + [blk[i, z, r] for i in range(18)]

    def collide_first(z, carry):
        zi = z + 1
        grads = gradient_tiles(p1, zi)
        dgrads = gradient_tiles(dp1, zi)
        for r in range(ROW_TILES):
            dens, psi = rho[zi, r], p1[zi, r]
            fluid = jnp.where(dens == 0.0, 0.0, 1.0)
            red = 0.5 * dens * (1.0 + psi)
            blue = 0.5 * dens * (1.0 - psi)
            alpha = red / (dens + (1.0 - fluid))
            beta = RECOLOURING_PACE * alpha * blue
            g = tuple(a[r] * (1.0 / 12.0) for a in grads)
            dg = tuple(a[r] * (1.0 / 12.0) for a in dgrads)
            gg, n = norm_parts(g)
            gdg = dot(g, dg)
            n2g = n * n * gdg
            dn = -n * n2g
            q = (SURFACE_TENSION * fluid) * n
            dq = -q * n2g
            for k in range(3):
                g1[k, zi, r] = g[k]
            sq, dsq = squares(g), squares_dot(g, dg)
            base = dens - q * gg * (1.0 / 3.0)
            dbase = (dq * gg + 2.0 * q * gdg) * (-1.0 / 3.0)
            ev = even_part(base, [q * v for v in sq])
            dev = even_part(dbase, [dq * v + q * d for v, d in zip(sq, dsq)])
            bn, bdn = beta * n, beta * dn
            od = odd_part([bn * v for v in g])
            dod = odd_part([bdn * v + bn * d for v, d in zip(g, dg)])
            for k in range(9):
                t_st[k, zi, r] = ev[k]
                dt_st[k, zi, r] = dev[k]
            pop[0, zi, r] = 12.0 * base
            dpop[0, zi, r] = 12.0 * dbase
            s = link(z, r)
            for first, rest, evens, odds in (
                (0, 12.0 * base, ev, od), (9, 12.0 * dbase, dev, dod)
            ):
                scaled = [alpha * v for v in evens]
                values = [alpha * rest]
                stay = []
                for k in range(9):
                    values += [scaled[k] + odds[k], scaled[k] - odds[k]]
                    stay += [s[2 * k + 1] * values[-2], s[2 * k + 2] * values[-1]]
                scatter_groups(acc.at[pl.ds(first, 9)], zi, r, values, total(stay))
        return carry

    lax.fori_loop(0, nz, collide_first, 0)

    def run_first(z, carry):
        zi = z + 1
        for ref, store in ((t_st, pop), (dt_st, dpop)):
            for i in range(1, 19):
                k = (i - 1) // 2
                arrived = moved(ref.at[k], zi, i, -1)
                for r in range(ROW_TILES):
                    blocked = blk[OPPOSITE[i] - 1, z, r] > 0.5
                    store[i, zi, r] = jnp.where(blocked, ref[k, zi, r], arrived[r])
        red_sum = gathered_sum(acc.at[pl.ds(0, 9)], zi)
        dred_sum = gathered_sum(acc.at[pl.ds(9, 9)], zi)
        for r in range(ROW_TILES):
            fluid = jnp.where(rho[zi, r] == 0.0, 0.0, 1.0)
            is_fluid = fluid > 0.5
            dens = total([pop[i, zi, r] for i in range(19)]) * (1.0 / 36.0)
            ddens = total([dpop[i, zi, r] for i in range(19)]) * (1.0 / 36.0)
            red = red_sum[r] * fluid * (1.0 / 36.0)
            dred = dred_sum[r] * fluid * (1.0 / 36.0)
            inv = 1.0 / (dens + (1.0 - fluid))
            psi = (2.0 * red - dens) * inv
            dpsi = (2.0 * dred - (1.0 + psi) * ddens) * inv
            for k, v in enumerate((dens, ddens, red, dred, inv, psi)):
                mac[k, zi, r] = v
            p2[zi, r] = jnp.where(is_fluid, psi, p1[zi, r])
            dp2[zi, r] = jnp.where(is_fluid, dpsi, dp1[zi, r])
        return carry

    lax.fori_loop(0, nz, run_first, 0)

    for k in range(36):
        for r in range(ROW_TILES):
            acc[k, 1, r] = zero_tile

    def collide_second(z, carry):
        zi = z + 1
        grads = gradient_tiles(p2, zi)
        dgrads = gradient_tiles(dp2, zi)
        for r in range(ROW_TILES):
            dens, ddens, red, dred, inv = [mac[k, zi, r] for k in range(5)]
            fluid = jnp.where(rho[zi, r] == 0.0, 0.0, 1.0)
            t = [pop[i, zi, r] for i in range(19)]
            dt = [dpop[i, zi, r] for i in range(19)]
            m = [v * (1.0 / 36.0) for v in first_moment(t)]
            dm = [v * (1.0 / 36.0) for v in first_moment(dt)]
            u = [inv * v for v in m]
            shrink = inv * ddens
            du = [inv * b - shrink * a for a, b in zip(u, dm)]
            g = tuple(a[r] * (1.0 / 12.0) for a in grads)
            dg = tuple(a[r] * (1.0 / 12.0) for a in dgrads)
            gg, n = norm_parts(g)
            gdg = dot(g, dg)
            n2g = n * n * gdg
            dn = -n * n2g
            q = (SURFACE_TENSION * fluid) * n
            dq = -q * n2g
            for k in range(3):
                g2s[k, zi, r] = g[k]
            base = RELAX_RATE * dens - (1.5 * RELAX_RATE) * dot(m, u) - q * gg * (1.0 / 3.0)
            dbase = (
                RELAX_RATE * ddens
                - (1.5 * RELAX_RATE) * (dot(dm, u) + dot(m, du))
                + (dq * gg + 2.0 * q * gdg) * (-1.0 / 3.0)
            )
            lin = odd_part([(3.0 * RELAX_RATE) * v for v in m])
            dlin = odd_part([(3.0 * RELAX_RATE) * v for v in dm])
            mq = [(4.5 * RELAX_RATE) * v for v in m]
            dmq = [(4.5 * RELAX_RATE) * v for v in dm]
            order = ((0, 0), (1, 1), (2, 2), (0, 1), (0, 2), (1, 2))
            sq, dsq = squares(g), squares_dot(g, dg)
            quad, dquad = [], []
            for k, (a, b) in enumerate(order):
                twice = 1.0 if a == b else 2.0
                flow = mq[a] * u[b]
                dflow = dmq[a] * u[b] + mq[a] * du[b]
                if a != b:
                    flow = 2.0 * flow
                    dflow = 2.0 * dflow
                quad.append(flow + q * sq[k])
                dquad.append(dflow + dq * sq[k] + q * dsq[k])
            ev, dev = even_part(base, quad), even_part(dbase, dquad)
            keep = 1.0 - RELAX_RATE
            after, dafter = [keep * t[0] + 12.0 * base], [keep * dt[0] + 12.0 * dbase]
            for k in range(9):
                after += [keep * t[2 * k + 1] + (ev[k] + lin[k]), keep * t[2 * k + 2] + (ev[k] - lin[k])]
                dafter += [
                    keep * dt[2 * k + 1] + (dev[k] + dlin[k]),
                    keep * dt[2 * k + 2] + (dev[k] - dlin[k]),
                ]
            alpha = red * inv
            dalpha = dred * inv - alpha * shrink
            blue, dblue = dens - red, ddens - dred
            beta = RECOLOURING_PACE * alpha * blue
            dbeta = RECOLOURING_PACE * (dalpha * blue + alpha * dblue)
            bn = beta * n
            dbn = dbeta * n + beta * dn
            od = odd_part([bn * v for v in g])
            dod = odd_part([dbn * v + bn * d for v, d in zip(g, dg)])
            reds, dreds = [alpha * after[0]], [dalpha * after[0] + alpha * dafter[0]]
            for i in range(1, 19):
                k = (i - 1) // 2
                side = od[k] if i % 2 else -od[k]
                dside = dod[k] if i % 2 else -dod[k]
                reds.append(alpha * after[i] + side)
                dreds.append(dalpha * after[i] + alpha * dafter[i] + dside)
            s = link(z, r)
            for k, values in enumerate((reds, dreds, after, dafter)):
                stay = total([s[i] * values[i] for i in range(1, 19)])
                scatter_groups(acc.at[pl.ds(9 * k, 9)], zi, r, values, stay)
        return carry

    lax.fori_loop(0, nz, collide_second, 0)

    for r in range(ROW_TILES):
        col[r] = zero_tile

    def final_phase(z, carry):
        zi = z + 1
        red_s, dred_s, dens_s, ddens_s = [gathered_sum(acc.at[pl.ds(9 * k, 9)], zi) for k in range(4)]
        for r in range(ROW_TILES):
            fluid = jnp.where(rho[zi, r] == 0.0, 0.0, 1.0)
            scale = fluid * (1.0 / 36.0)
            dens = dens_s[r] * scale
            inv = 1.0 / (dens + (1.0 - fluid))
            psi = (2.0 * (red_s[r] * scale) - dens) * inv
            a = 2.0 * (scale * inv)
            b = -(scale * inv) * (1.0 + psi)
            a3[zi, r] = a
            b3[zi, r] = b
            col[r] = col[r] + (a * dred_s[r] + b * ddens_s[r])
        return carry

    lax.fori_loop(0, nz, final_phase, 0)
    read_ref[...] = jnp.take_along_axis(col[0, :, :HALF], map_ref[...], axis=1)

    def seed(z, carry):
        zi = z + 1
        for r in range(ROW_TILES):
            column = col[r] * cnt[r]
            a3[zi, r] = a3[zi, r] * column
            b3[zi, r] = b3[zi, r] * column
        return carry

    lax.fori_loop(0, nz, seed, 0)

    def toward_gradient(g, fluid, zeroth, second, first, beta):
        gg, n = norm_parts(g)
        trace = zeroth * (1.0 / 3.0)
        shifted = [second[0] - trace, second[1] - trace, second[2] - trace] + list(second[3:])
        yg = times(shifted, g)
        gf = dot(g, first)
        nbar = (SURFACE_TENSION * fluid) * dot(g, yg) + beta * gf
        two_q = (2.0 * SURFACE_TENSION * fluid) * n
        bn = beta * n
        fall = nbar * n * n * n
        return [two_q * y + bn * f - fall * v for y, f, v in zip(yg, first, g)], n * gf

    def back_second(z, carry):
        zi = z + 1
        ahead_r = all_moved(a3, zi)
        ahead_t = all_moved(b3, zi)
        for r in range(ROW_TILES):
            s = link(z, r)
            own_r, own_t = a3[zi, r], b3[zi, r]
            dens, _, red, _, inv = [mac[k, zi, r] for k in range(5)]
            fluid = jnp.where(rho[zi, r] == 0.0, 0.0, 1.0)
            alpha = red * inv
            blue = dens - red
            beta = RECOLOURING_PACE * alpha * blue
            r_hat, hat = [own_r], [own_t + alpha * own_r]
            for i in range(1, 19):
                blocked = s[i] > 0.5
                r_i = jnp.where(blocked, own_r, ahead_r[i][r])
                t_i = jnp.where(blocked, own_t, ahead_t[i][r])
                r_hat.append(r_i)
                hat.append(t_i + alpha * r_i)
            t = [pop[i, zi, r] for i in range(19)]
            m = [v * (1.0 / 36.0) for v in first_moment(t)]
            u = [inv * v for v in m]
            g = tuple(g2s[k, zi, r] for k in range(3))
            gg, n = norm_parts(g)
            q = (SURFACE_TENSION * fluid) * n
            h0, h2 = weighted_even(hat[0], pair_sums(hat))
            h1 = weighted_first(hat)
            k0, k2 = weighted_even(r_hat[0], pair_sums(r_hat))
            k1 = weighted_first(r_hat)
            bars, n_gk = toward_gradient(g, fluid, h0, h2, k1, beta)
            for k in range(3):
                gbar[k, zi, r] = bars[k]
            uu = 1.5 * RELAX_RATE
            flow = [(4.5 * RELAX_RATE) * k2[j] - (uu * k0 if j < 3 else 0.0) for j in range(6)]
            surf = [k2[j] - (k0 * (1.0 / 3.0) if j < 3 else 0.0) for j in range(6)]
            alpha_bar = (
                (1.0 - RELAX_RATE) * total([a * b for a, b in zip(r_hat, t)])
                + RELAX_RATE * dens * k0
                + (3.0 * RELAX_RATE) * dot(m, k1)
                + dot(m, times(flow, u))
                + q * dot(g, times(surf, g))
            )
            alpha_bar = alpha_bar + RECOLOURING_PACE * blue * n_gk
            blue_bar = RECOLOURING_PACE * alpha * n_gk
            flow_h = [(4.5 * RELAX_RATE) * h2[j] - (uu * h0 if j < 3 else 0.0) for j in range(6)]
            xu = times(flow_h, u)
            red_bar = inv * alpha_bar - blue_bar
            dens_bar = RELAX_RATE * h0 - dot(u, xu) + blue_bar - alpha * inv * alpha_bar
            adj[19, zi, r] = red_bar
            adj[20, zi, r] = dens_bar
            for k in range(3):
                adj[21 + k, zi, r] = ((3.0 * RELAX_RATE) * h1[k] + 2.0 * xu[k]) * (1.0 / 36.0)
            for i in range(19):
                adj[i, zi, r] = hat[i]
        return carry

    lax.fori_loop(0, nz, back_second, 0)

    def back_phase(z, carry):
        zi = z + 1
        field = gradient_back([gbar.at[k] for k in range(3)], zi)
        for r in range(ROW_TILES):
            fluid = jnp.where(rho[zi, r] == 0.0, 0.0, 1.0)
            inv, psi = mac[4, zi, r], mac[5, zi, r]
            bar = field[r] * (-1.0 / 12.0)
            pbar2[zi, r] = bar
            psi_bar = fluid * bar * inv
            red_bar = adj[19, zi, r] + 2.0 * psi_bar
            dens_bar = (adj[20, zi, r] - (1.0 + psi) * psi_bar) * (1.0 / 36.0)
            push = odd_part([adj[21 + k, zi, r] for k in range(3)])
            push[:3] = [adj[21 + k, zi, r] for k in range(3)]
            keep = 1.0 - RELAX_RATE
            adj[19, zi, r] = red_bar * (1.0 / 36.0)
            adj[0, zi, r] = keep * adj[0, zi, r] + dens_bar
            for k in range(9):
                adj[2 * k + 1, zi, r] = keep * adj[2 * k + 1, zi, r] + (dens_bar + push[k])
                adj[2 * k + 2, zi, r] = keep * adj[2 * k + 2, zi, r] + (dens_bar - push[k])
        return carry

    lax.fori_loop(0, nz, back_phase, 0)

    def back_first(z, carry):
        zi = z + 1
        ahead = [None] + [moved(adj.at[i], zi, i, 1) for i in range(1, 19)]
        ahead_r = all_moved(adj.at[19], zi)
        for r in range(ROW_TILES):
            s = link(z, r)
            dens, psi = rho[zi, r], p1[zi, r]
            fluid = jnp.where(dens == 0.0, 0.0, 1.0)
            red = 0.5 * dens * (1.0 + psi)
            blue = 0.5 * dens * (1.0 - psi)
            alpha = red / (dens + (1.0 - fluid))
            beta = RECOLOURING_PACE * alpha * blue
            own = adj[19, zi, r]
            r_hat, hat = [own], [adj[0, zi, r] + alpha * own]
            for i in range(1, 19):
                blocked = s[i] > 0.5
                r_i = jnp.where(blocked, own, ahead_r[i][r])
                r_hat.append(r_i)
                hat.append(jnp.where(blocked, adj[OPPOSITE[i], zi, r], ahead[i][r]) + alpha * r_i)
            h0, h2 = weighted_even(hat[0], pair_sums(hat))
            g = tuple(g1[k, zi, r] for k in range(3))
            bars, _ = toward_gradient(g, fluid, h0, h2, weighted_first(r_hat), beta)
            for k in range(3):
                gbar[k, zi, r] = bars[k]
        return carry

    lax.fori_loop(0, nz, back_first, 0)

    for zl in range(local_z):
        zi = 1 + thick * local_z + zl
        field = gradient_back([gbar.at[k] for k in range(3)], zi)
        bar = pbar2[zi, 0] + field[0] * (-1.0 / 12.0)
        bar = jnp.where(rho[zi, 0] == 0.0, bar, 0.0)
        out_ref[zl] = bar[:, :HALF]


def pack_kernel(local_z, solid_ref, labels_ref, density_ref, wet_ref, dir_ref, map_ref, out_ref):
    for z in range(local_z):
        solid = solid_ref[z].astype(jnp.float32)
        label = labels_ref[z].astype(jnp.float32)
        fluid = 1.0 - solid
        red = density_ref[z] * label * fluid
        blue = density_ref[z] * (1.0 - label) * fluid
        psi = (red - blue) / (red + blue + solid)
        out_ref[z] = red + blue
        out_ref[local_z + z] = fluid * psi + solid * wet_ref[z]
        out_ref[2 * local_z + z] = solid * dir_ref[z]
    pixels = map_ref[...]
    lane = lax.broadcasted_iota(jnp.int32, pixels.shape, 1)
    counts = jnp.zeros(pixels.shape, jnp.int32)
    for k in range(pixels.shape[1]):
        turned = pltpu.roll(pixels, k, 1) if k else pixels
        counts = counts + (turned == lane).astype(jnp.int32)
    out_ref[3 * local_z] = counts.astype(jnp.float32)


def one_exchange(solid, labels, density, wettability, direction, pixel_map):
    local_z = solid.shape[0]
    planes, slabs = lax.axis_size("plane"), lax.axis_size("thick")
    nz = local_z * slabs
    per = 3 * local_z + 1
    vmem = pl.BlockSpec(memory_space=pltpu.VMEM)
    packed = pl.pallas_call(
        functools.partial(pack_kernel, local_z),
        out_shape=jax.ShapeDtypeStruct((per, 8, HALF), jnp.float32),
        in_specs=[vmem] * 6,
        out_specs=vmem,
    )(solid[:, 0], labels[:, 0], density[:, 0], wettability[:, 0], direction[:, 0], pixel_map[0])

    def send(array, target):
        route = []
        for b in range(planes):
            for t in range(slabs):
                to_b, to_t = target(b, t)
                route.append((b * slabs + t, (to_b % planes) * slabs + to_t))
        return lax.ppermute(array, ("plane", "thick"), route)

    beside_z = send(packed, lambda b, t: (b, 1 - t))
    beside_y = send(packed, lambda b, t: (b ^ 1, t))
    beside_zy = send(packed, lambda b, t: (b ^ 1, 1 - t))
    quad = jnp.concatenate([beside_y, beside_zy, packed, beside_z])
    above = send(quad, lambda b, t: (b + 2, t))
    below = send(quad, lambda b, t: (b - 2, t))
    corner = send(quad[: 2 * per], lambda b, t: (b + 4 if b % 2 == 0 else b - 4, t))

    def field(*lead):
        return pltpu.VMEM(lead + (ROW_TILES, 8, WIDE), jnp.float32)

    padded = nz + 2
    return pl.pallas_call(
        functools.partial(main_kernel, nz, local_z),
        out_shape=(
            jax.ShapeDtypeStruct((local_z, 8, HALF), jnp.float32),
            jax.ShapeDtypeStruct((8, HALF), jnp.float32),
        ),
        in_specs=[vmem] * 5,
        out_specs=(vmem, vmem),
        scratch_shapes=[
            field(padded), field(padded), field(padded), field(),
            field(18, nz), field(9, padded), field(9, padded), field(36, padded),
            field(19, padded), field(19, padded), field(6, padded),
            field(padded), field(padded), field(3, padded), field(3, padded),
            field(padded), field(padded), field(), field(24, padded), field(3, padded),
            field(padded),
        ],
        compiler_params=pltpu.CompilerParams(vmem_limit_bytes=56 * 1024 * 1024),
    )(quad, above, below, corner, pixel_map[0])


def fits_one_exchange(mesh, solid):
    return mesh.shape["plane"] == 2 * NBX and mesh.shape["thick"] == 2 and solid.shape[2:] == (8, HALF)


def solution(mesh):
    specs = (P("thick", "plane", None, None),) * 5 + (P("plane", None, None),)
    out_specs = (P("thick", "plane", None, None), P("plane", None, None))

    def program(solid, *rest):
        def with_bricks(*blocks):
            curvature, readings = one_exchange(*blocks)
            return curvature[:, None], readings[None]

        body = with_bricks if fits_one_exchange(mesh, solid) else per_device
        return jax.shard_map(
            body, mesh=mesh, in_specs=specs, out_specs=out_specs, check_vma=False
        )(solid, *rest)

    return program
```

profile of v0, /device:TPU:0, one launch (start us, length us, event | category | flops | bytes accessed | tf_op | source)
XLA Modules:
  0.0 35.7 jit_solution(2993803186428285891)
XLA Ops:
  0.6 1.6 %shard_map.77 = f32[7,8,128]{2,1,0:T(8,128)} custom-call(s32[2,8,128]{2,1,0:T(8,128)} %bitcast.12, s32[2,8,128]{2,1,0:T(8,128)} %bitcast.13, f32[2,8,128]{2,1,0:T(8,128)} %bitcast.14, f32[2,8,128]{2,1,0:T(8,128)} %bitcast.15, f32[2,8,128]{2,1,0:T(8,128)} %bitcast.16, s32[8,128]{1,0:T(8,128)} %bitcast.10), custom_call_target="tpu_custom_call" | custom-call | tf_op jit(solution)/shard_map/pallas_call | solution.py:946
  2.2 2.9 %collective-permute-start.2 = (f32[7,8,128]{2,1,0:T(8,128)}, f32[7,8,128]{2,1,0:T(8,128)S(1)}, u32[]{:S(2)}, u32[]{:S(2)}) collective-permute-start(f32[7,8,128]{2,1,0:T(8,128)} %shard_map.77), channel_id=1, source_target_pairs={{0,1},{1,0},{2,3},{3,2},{4,5},{5,4},{6,7},{7,6},{8,9},{9,8},{10,11... | collective-permute-start | bytes 86024 | tf_op jit(solution)/shard_map/ppermute | solution.py:959
  5.2 0.0 collective-permute-start.1
  5.2 0.1 collective-permute-start
  5.3 1.9 %collective-permute-done.2 = f32[7,8,128]{2,1,0:T(8,128)S(1)} collective-permute-done((f32[7,8,128]{2,1,0:T(8,128)}, f32[7,8,128]{2,1,0:T(8,128)S(1)}, u32[]{:S(2)}, u32[]{:S(2)}) %collective-permute-start.2) | collective-permute-done | bytes 28704 | tf_op jit(solution)/shard_map/ppermute | solution.py:959
  7.2 1.5 %collective-permute-done.1 = f32[7,8,128]{2,1,0:T(8,128)S(1)} collective-permute-done((f32[7,8,128]{2,1,0:T(8,128)}, f32[7,8,128]{2,1,0:T(8,128)S(1)}, u32[]{:S(2)}, u32[]{:S(2)}) %collective-permute-start.1) | collective-permute-done | bytes 28704 | tf_op jit(solution)/shard_map/ppermute | solution.py:959
  8.7 0.0 collective-permute-done
  8.7 0.8 %pad_maximum_fusion.q_ref = f32[28,8,128]{2,1,0:T(8,128)S(1)} fusion(f32[7,8,128]{2,1,0:T(8,128)S(1)} %collective-permute-done.2, f32[7,8,128]{2,1,0:T(8,128)} %shard_map.77, f32[7,8,128]{2,1,0:T(8,128)S(1)} %collective-permute-done.1, f32[7,8,128]{2,1,0:T(8,128)S(1)} %collective-permute-done), kind=kLoop, calls=%fused_computation | loop fusion | flops 86016 | bytes 229376 | tf_op jit(solution)/shard_map/concatenate | solution.py:964
  9.5 0.0 copy-start
  9.5 4.6 %collective-permute-start.4 = (f32[28,8,128]{2,1,0:T(8,128)S(1)}, f32[28,8,128]{2,1,0:T(8,128)S(1)}, u32[]{:S(2)}, u32[]{:S(2)}) collective-permute-start(f32[28,8,128]{2,1,0:T(8,128)S(1)} %pad_maximum_fusion.q_ref), channel_id=1, source_target_pairs={{0,28},{1,29},{2,30},{3,31},{4,0},{5,1},{6,2},{7,3},{8,4},{9,5},{1... | collective-permute-start | bytes 344072 | tf_op jit(solution)/shard_map/ppermute | solution.py:959
  14.1 0.0 collective-permute-start.3
  14.1 0.1 collective-permute-start.5
  14.2 6.0 %collective-permute-done.5.sl_ref = f32[14,8,128]{2,1,0:T(8,128)S(1)} collective-permute-done((f32[14,8,128]{2,1,0:T(8,128)S(1)}, f32[14,8,128]{2,1,0:T(8,128)S(1)}, u32[]{:S(2)}, u32[]{:S(2)}) %collective-permute-start.5) | collective-permute-done | bytes 57376 | tf_op jit(solution)/shard_map/ppermute | solution.py:959
  20.1 0.0 copy-start.3
  20.1 0.0 collective-permute-done.4.qp_ref
  20.1 0.0 copy-start.1
  20.1 1.9 %collective-permute-done.3.qm_ref = f32[28,8,128]{2,1,0:T(8,128)S(1)} collective-permute-done((f32[28,8,128]{2,1,0:T(8,128)S(1)}, f32[28,8,128]{2,1,0:T(8,128)S(1)}, u32[]{:S(2)}, u32[]{:S(2)}) %collective-permute-start.3) | collective-permute-done | bytes 114720 | tf_op jit(solution)/shard_map/ppermute | solution.py:959
  22.0 0.0 copy-done
  22.0 0.0 copy-done.3
  22.0 0.0 copy-done.1
  22.0 0.0 copy-start.2
  22.0 0.6 %copy-done.2 = f32[28,8,128]{2,1,0:T(8,128)} copy-done((f32[28,8,128]{2,1,0:T(8,128)}, f32[28,8,128]{2,1,0:T(8,128)S(1)}, u32[]{:S(2)}) %copy-start.2) | copy-done | bytes 114712
  22.7 13.0 %shard_map.78 = (f32[2,8,128]{2,1,0:T(8,128)}, f32[8,128]{1,0:T(8,128)}) custom-call(f32[28,8,128]{2,1,0:T(8,128)} %copy-done, f32[28,8,128]{2,1,0:T(8,128)} %copy-done.2, f32[28,8,128]{2,1,0:T(8,128)} %copy-done.1, f32[14,8,128]{2,1,0:T(8,128)} %copy-done.3, s32[8,128]{1,0:T(8,128)} %bitcast.11), custom_call_target="tpu_custom_call" | custom-call | tf_op jit(solution)/shard_map/pallas_call | solution.py:973
  (1 shorter events, 0.0 us)
Async XLA Ops:
  2.2 5.0 %collective-permute-start.2 = (f32[7,8,128]{2,1,0:T(8,128)}, f32[7,8,128]{2,1,0:T(8,128)S(1)}, u32[]{:S(2)}, u32[]{:S(2)}) collective-permute-start(f32[7,8,128]{2,1,0:T(8,128)} %shard_map.77), channel_id=1, source_target_pairs={{0,1},{1,0},{2,3},{3,2},{4,5},{5,4},{6,7},{7,6},{8,9},{9,8},{10,11... | collective-permute-start | bytes 86024 | tf_op jit(solution)/shard_map/ppermute | solution.py:959
  5.2 3.5 %collective-permute-start.1 = (f32[7,8,128]{2,1,0:T(8,128)}, f32[7,8,128]{2,1,0:T(8,128)S(1)}, u32[]{:S(2)}, u32[]{:S(2)}) collective-permute-start(f32[7,8,128]{2,1,0:T(8,128)} %shard_map.77), channel_id=1, source_target_pairs={{0,3},{1,2},{2,1},{3,0},{4,7},{5,6},{6,5},{7,4},{8,11},{9,10},{10,... | collective-permute-start | bytes 86024 | tf_op jit(solution)/shard_map/ppermute | solution.py:959
  5.2 3.5 %collective-permute-start = (f32[7,8,128]{2,1,0:T(8,128)}, f32[7,8,128]{2,1,0:T(8,128)S(1)}, u32[]{:S(2)}, u32[]{:S(2)}) collective-permute-start(f32[7,8,128]{2,1,0:T(8,128)} %shard_map.77), channel_id=1, source_target_pairs={{0,2},{1,3},{2,0},{3,1},{4,6},{5,7},{6,4},{7,5},{8,10},{9,11},{10,... | collective-permute-start | bytes 86024 | tf_op jit(solution)/shard_map/ppermute | solution.py:959
  9.5 12.5 %copy-start = (f32[28,8,128]{2,1,0:T(8,128)}, f32[28,8,128]{2,1,0:T(8,128)S(1)}, u32[]{:S(2)}) copy-start(f32[28,8,128]{2,1,0:T(8,128)S(1)} %pad_maximum_fusion.q_ref) | copy-start | bytes 344068
  9.5 10.7 %collective-permute-start.4 = (f32[28,8,128]{2,1,0:T(8,128)S(1)}, f32[28,8,128]{2,1,0:T(8,128)S(1)}, u32[]{:S(2)}, u32[]{:S(2)}) collective-permute-start(f32[28,8,128]{2,1,0:T(8,128)S(1)} %pad_maximum_fusion.q_ref), channel_id=1, source_target_pairs={{0,28},{1,29},{2,30},{3,31},{4,0},{5,1},{6,2},{7,3},{8,4},{9,5},{1... | collective-permute-start | bytes 344072 | tf_op jit(solution)/shard_map/ppermute | solution.py:959
  14.1 7.9 %collective-permute-start.3 = (f32[28,8,128]{2,1,0:T(8,128)S(1)}, f32[28,8,128]{2,1,0:T(8,128)S(1)}, u32[]{:S(2)}, u32[]{:S(2)}) collective-permute-start(f32[28,8,128]{2,1,0:T(8,128)S(1)} %pad_maximum_fusion.q_ref), channel_id=1, source_target_pairs={{0,4},{1,5},{2,6},{3,7},{4,8},{5,9},{6,10},{7,11},{8,12},{9,13},{1... | collective-permute-start | bytes 344072 | tf_op jit(solution)/shard_map/ppermute | solution.py:959
  14.1 6.0 %collective-permute-start.5 = (f32[14,8,128]{2,1,0:T(8,128)S(1)}, f32[14,8,128]{2,1,0:T(8,128)S(1)}, u32[]{:S(2)}, u32[]{:S(2)}) collective-permute-start(f32[14,8,128]{2,1,0:T(8,128)S(1)} %pad_maximum_fusion.1), channel_id=1, source_target_pairs={{0,8},{1,9},{2,26},{3,27},{4,12},{5,13},{6,30},{7,31},{8,16},{9,17... | collective-permute-start | bytes 172040 | tf_op jit(solution)/shard_map/ppermute | solution.py:959
  20.1 1.9 %copy-start.3 = (f32[14,8,128]{2,1,0:T(8,128)}, f32[14,8,128]{2,1,0:T(8,128)S(1)}, u32[]{:S(2)}) copy-start(f32[14,8,128]{2,1,0:T(8,128)S(1)} %collective-permute-done.5.sl_ref) | copy-start | bytes 172036
  20.1 1.9 %copy-start.1 = (f32[28,8,128]{2,1,0:T(8,128)}, f32[28,8,128]{2,1,0:T(8,128)S(1)}, u32[]{:S(2)}) copy-start(f32[28,8,128]{2,1,0:T(8,128)S(1)} %collective-permute-done.4.qp_ref) | copy-start | bytes 344068
  22.0 0.6 %copy-start.2 = (f32[28,8,128]{2,1,0:T(8,128)}, f32[28,8,128]{2,1,0:T(8,128)S(1)}, u32[]{:S(2)}) copy-start(f32[28,8,128]{2,1,0:T(8,128)S(1)} %collective-permute-done.3.qm_ref) | copy-start | bytes 344068
where the time goes:
time: 36 us; the launch traced here: 35.7 us
  Pallas kernels  14.6 us (41%)
  waiting for transfers between devices  11.2 us (31%)
  starting transfers between devices  7.76 us (22%)
  other arithmetic  0.76 us (2%)
  between operations  0.67 us (2%)
  local copies, waits for them, and re-layouts  0.65 us (2%)
    pallas_call x1, Pallas kernels, one_exchange(): pl.pallas_call(functools.partial(main_kernel, nz, local_z), out_shape=(ja...  13 us
    ppermute x6, waiting for transfers between devices, send(): return lax.ppermute(array, ('plane', 'thick'), route)  11.2 us
    ppermute x6, starting transfers between devices, send(): return lax.ppermute(array, ('plane', 'thick'), route)  7.76 us
    pallas_call x1, Pallas kernels, one_exchange(): pl.pallas_call(functools.partial(pack_kernel, local_z), out_shape=jax.Sha...  1.58 us
    concatenate x2, other arithmetic, one_exchange(): quad = jnp.concatenate([beside_y, beside_zy, packed, beside_z])  0.76 us
  transfers between devices with their start and end apart: 6, of which 4 were waited for; matrix products, arithmetic and copies ran while one was open for 0% of the time, Pallas kernels for 0%

commit v1 on v0

--- a/solution.py
+++ b/solution.py
@@ -590,7 +590,7 @@
                         blk[i - 1, z, r] = jnp.maximum(tiles[r], here[r])
         return carry
 
-    lax.fori_loop(0, nz, links, 0)
+    lax.fori_loop(0, nz, links, 0, unroll=True)
 
     def link(z, r):
         return [None] + [blk[i, z, r] for i in range(18)]
@@ -642,7 +642,7 @@
                 scatter_groups(acc.at[pl.ds(first, 9)], zi, r, values, total(stay))
         return carry
 
-    lax.fori_loop(0, nz, collide_first, 0)
+    lax.fori_loop(0, nz, collide_first, 0, unroll=True)
 
     def run_first(z, carry):
         zi = z + 1
@@ -671,7 +671,7 @@
             dp2[zi, r] = jnp.where(is_fluid, dpsi, dp1[zi, r])
         return carry
 
-    lax.fori_loop(0, nz, run_first, 0)
+    lax.fori_loop(0, nz, run_first, 0, unroll=True)
 
     for k in range(36):
         for r in range(ROW_TILES):
@@ -754,7 +754,7 @@
                 scatter_groups(acc.at[pl.ds(9 * k, 9)], zi, r, values, stay)
         return carry
 
-    lax.fori_loop(0, nz, collide_second, 0)
+    lax.fori_loop(0, nz, collide_second, 0, unroll=True)
 
     for r in range(ROW_TILES):
         col[r] = zero_tile
@@ -775,7 +775,7 @@
             col[r] = col[r] + (a * dred_s[r] + b * ddens_s[r])
         return carry
 
-    lax.fori_loop(0, nz, final_phase, 0)
+    lax.fori_loop(0, nz, final_phase, 0, unroll=True)
     read_ref[...] = jnp.take_along_axis(col[0, :, :HALF], map_ref[...], axis=1)
 
     def seed(z, carry):
@@ -786,7 +786,7 @@
             b3[zi, r] = b3[zi, r] * column
         return carry
 
-    lax.fori_loop(0, nz, seed, 0)
+    lax.fori_loop(0, nz, seed, 0, unroll=True)
 
     def toward_gradient(g, fluid, zeroth, second, first, beta):
         gg, n = norm_parts(g)
@@ -856,7 +856,7 @@
                 adj[i, zi, r] = hat[i]
         return carry
 
-    lax.fori_loop(0, nz, back_second, 0)
+    lax.fori_loop(0, nz, back_second, 0, unroll=True)
 
     def back_phase(z, carry):
         zi = z + 1
@@ -879,7 +879,7 @@
                 adj[2 * k + 2, zi, r] = keep * adj[2 * k + 2, zi, r] + (dens_bar - push[k])
         return carry
 
-    lax.fori_loop(0, nz, back_phase, 0)
+    lax.fori_loop(0, nz, back_phase, 0, unroll=True)
 
     def back_first(z, carry):
         zi = z + 1
@@ -907,7 +907,7 @@
                 gbar[k, zi, r] = bars[k]
         return carry
 
-    lax.fori_loop(0, nz, back_first, 0)
+    lax.fori_loop(0, nz, back_first, 0, unroll=True)
 
     for zl in range(local_z):
         zi = 1 + thick * local_z + zl
@@ -986,7 +986,7 @@
             field(padded), field(padded), field(), field(24, padded), field(3, padded),
             field(padded),
         ],
-        compiler_params=pltpu.CompilerParams(vmem_limit_bytes=56 * 1024 * 1024),
+        compiler_params=pltpu.CompilerParams(vmem_limit_bytes=30 * 1024 * 1024),
     )(quad, above, below, corner, pixel_map[0])
 
 

time: 36 us -> 31.9 us (0.89)
  Pallas kernels: 14.6 us -> 11.3 us
  local copies, waits for them, and re-layouts: 0.65 us -> 0.01 us
    pallas_call x1, Pallas kernels: 13 us -> 9.68 us  [one_exchange(): pl.pallas_call(functools.partial(main_kernel, nz, local_z), out_shape=(ja...]
    unnamed x8 -> x2, local copies, waits for them, and re-layouts: 0.65 us -> 0.01 us
where the time goes in v1:
time: 31.9 us; the launch traced here: 31.7 us
  Pallas kernels  11.3 us (35%)
  waiting for transfers between devices  11.3 us (35%)
  starting transfers between devices  7.76 us (24%)
  other arithmetic  0.76 us (2%)
  between operations  0.65 us (2%)
    ppermute x6, waiting for transfers between devices, send(): return lax.ppermute(array, ('plane', 'thick'), route)  11.3 us
    pallas_call x1, Pallas kernels, one_exchange(): pl.pallas_call(functools.partial(main_kernel, nz, local_z), out_shape=(ja...  9.68 us
    ppermute x6, starting transfers between devices, send(): return lax.ppermute(array, ('plane', 'thick'), route)  7.76 us
    pallas_call x1, Pallas kernels, one_exchange(): pl.pallas_call(functools.partial(pack_kernel, local_z), out_shape=jax.Sha...  1.57 us
    concatenate x2, other arithmetic, one_exchange(): quad = jnp.concatenate([beside_y, beside_zy, packed, beside_z])  0.76 us
  transfers between devices with their start and end apart: 6, of which 4 were waited for; matrix products, arithmetic and copies ran while one was open for 0% of the time, Pallas kernels for 0%

profile of v1, /device:TPU:0, one launch (start us, length us, event | category | flops | bytes accessed | tf_op | source)
XLA Modules:
  0.0 31.7 jit_solution(13064180806067220349)
XLA Ops:
  0.6 1.6 %shard_map.77 = f32[7,8,128]{2,1,0:T(8,128)} custom-call(s32[2,8,128]{2,1,0:T(8,128)} %bitcast.12, s32[2,8,128]{2,1,0:T(8,128)} %bitcast.13, f32[2,8,128]{2,1,0:T(8,128)} %bitcast.14, f32[2,8,128]{2,1,0:T(8,128)} %bitcast.15, f32[2,8,128]{2,1,0:T(8,128)} %bitcast.16, s32[8,128]{1,0:T(8,128)} %bitcast.10), custom_call_target="tpu_custom_call" | custom-call | tf_op jit(solution)/shard_map/pallas_call | solution.py:946
  2.2 2.9 %collective-permute-start.2 = (f32[7,8,128]{2,1,0:T(8,128)}, f32[7,8,128]{2,1,0:T(8,128)S(1)}, u32[]{:S(2)}, u32[]{:S(2)}) collective-permute-start(f32[7,8,128]{2,1,0:T(8,128)} %shard_map.77), channel_id=1, source_target_pairs={{0,1},{1,0},{2,3},{3,2},{4,5},{5,4},{6,7},{7,6},{8,9},{9,8},{10,11... | collective-permute-start | bytes 86024 | tf_op jit(solution)/shard_map/ppermute | solution.py:959
  5.1 0.0 collective-permute-start.1
  5.1 0.1 collective-permute-start
  5.3 1.9 %collective-permute-done.2 = f32[7,8,128]{2,1,0:T(8,128)S(1)} collective-permute-done((f32[7,8,128]{2,1,0:T(8,128)}, f32[7,8,128]{2,1,0:T(8,128)S(1)}, u32[]{:S(2)}, u32[]{:S(2)}) %collective-permute-start.2) | collective-permute-done | bytes 28704 | tf_op jit(solution)/shard_map/ppermute | solution.py:959
  7.2 1.5 %collective-permute-done.1 = f32[7,8,128]{2,1,0:T(8,128)S(1)} collective-permute-done((f32[7,8,128]{2,1,0:T(8,128)}, f32[7,8,128]{2,1,0:T(8,128)S(1)}, u32[]{:S(2)}, u32[]{:S(2)}) %collective-permute-start.1) | collective-permute-done | bytes 28704 | tf_op jit(solution)/shard_map/ppermute | solution.py:959
  8.7 0.0 collective-permute-done
  8.7 0.8 %pad_maximum_fusion.q_ref = f32[28,8,128]{2,1,0:T(8,128)S(1)} fusion(f32[7,8,128]{2,1,0:T(8,128)S(1)} %collective-permute-done.2, f32[7,8,128]{2,1,0:T(8,128)} %shard_map.77, f32[7,8,128]{2,1,0:T(8,128)S(1)} %collective-permute-done.1, f32[7,8,128]{2,1,0:T(8,128)S(1)} %collective-permute-done), kind=kLoop, calls=%fused_computation | loop fusion | flops 86016 | bytes 229376 | tf_op jit(solution)/shard_map/concatenate | solution.py:964
  9.5 0.0 copy-start
  9.5 4.6 %collective-permute-start.4 = (f32[28,8,128]{2,1,0:T(8,128)S(1)}, f32[28,8,128]{2,1,0:T(8,128)S(1)}, u32[]{:S(2)}, u32[]{:S(2)}) collective-permute-start(f32[28,8,128]{2,1,0:T(8,128)S(1)} %pad_maximum_fusion.q_ref), channel_id=1, source_target_pairs={{0,28},{1,29},{2,30},{3,31},{4,0},{5,1},{6,2},{7,3},{8,4},{9,5},{1... | collective-permute-start | bytes 344072 | tf_op jit(solution)/shard_map/ppermute | solution.py:959
  14.1 0.0 collective-permute-start.3
  14.1 0.1 collective-permute-start.5
  14.1 6.0 %collective-permute-done.5.sl_ref = f32[14,8,128]{2,1,0:T(8,128)S(1)} collective-permute-done((f32[14,8,128]{2,1,0:T(8,128)S(1)}, f32[14,8,128]{2,1,0:T(8,128)S(1)}, u32[]{:S(2)}, u32[]{:S(2)}) %collective-permute-start.5) | collective-permute-done | bytes 57376 | tf_op jit(solution)/shard_map/ppermute | solution.py:959
  20.1 0.0 collective-permute-done.4.qp_ref
  20.1 1.9 %collective-permute-done.3.qm_ref = f32[28,8,128]{2,1,0:T(8,128)S(1)} collective-permute-done((f32[28,8,128]{2,1,0:T(8,128)S(1)}, f32[28,8,128]{2,1,0:T(8,128)S(1)}, u32[]{:S(2)}, u32[]{:S(2)}) %collective-permute-start.3) | collective-permute-done | bytes 114720 | tf_op jit(solution)/shard_map/ppermute | solution.py:959
  22.0 0.0 copy-done
  22.0 9.7 %shard_map.78 = (f32[2,8,128]{2,1,0:T(8,128)}, f32[8,128]{1,0:T(8,128)}) custom-call(f32[28,8,128]{2,1,0:T(8,128)S(1)} %pad_maximum_fusion.q_ref, f32[28,8,128]{2,1,0:T(8,128)S(1)} %collective-permute-done.3.qm_ref, f32[28,8,128]{2,1,0:T(8,128)S(1)} %collective-permute-done.4.qp_ref, f32[14,8,128]{2,1,0:T(8,128)S(1)} %collective-permute-done.5.sl_ref, ...), custom_call_target="tpu_custom_call" | custom-call | tf_op jit(solution)/shard_map/pallas_call | solution.py:973
  (1 shorter events, 0.0 us)
Async XLA Ops:
  2.2 5.0 %collective-permute-start.2 = (f32[7,8,128]{2,1,0:T(8,128)}, f32[7,8,128]{2,1,0:T(8,128)S(1)}, u32[]{:S(2)}, u32[]{:S(2)}) collective-permute-start(f32[7,8,128]{2,1,0:T(8,128)} %shard_map.77), channel_id=1, source_target_pairs={{0,1},{1,0},{2,3},{3,2},{4,5},{5,4},{6,7},{7,6},{8,9},{9,8},{10,11... | collective-permute-start | bytes 86024 | tf_op jit(solution)/shard_map/ppermute | solution.py:959
  5.1 3.5 %collective-permute-start.1 = (f32[7,8,128]{2,1,0:T(8,128)}, f32[7,8,128]{2,1,0:T(8,128)S(1)}, u32[]{:S(2)}, u32[]{:S(2)}) collective-permute-start(f32[7,8,128]{2,1,0:T(8,128)} %shard_map.77), channel_id=1, source_target_pairs={{0,3},{1,2},{2,1},{3,0},{4,7},{5,6},{6,5},{7,4},{8,11},{9,10},{10,... | collective-permute-start | bytes 86024 | tf_op jit(solution)/shard_map/ppermute | solution.py:959
  5.1 3.5 %collective-permute-start = (f32[7,8,128]{2,1,0:T(8,128)}, f32[7,8,128]{2,1,0:T(8,128)S(1)}, u32[]{:S(2)}, u32[]{:S(2)}) collective-permute-start(f32[7,8,128]{2,1,0:T(8,128)} %shard_map.77), channel_id=1, source_target_pairs={{0,2},{1,3},{2,0},{3,1},{4,6},{5,7},{6,4},{7,5},{8,10},{9,11},{10,... | collective-permute-start | bytes 86024 | tf_op jit(solution)/shard_map/ppermute | solution.py:959
  9.5 12.5 %copy-start = (s32[1,8,128]{2,1,0:T(8,128)S(1)}, s32[1,8,128]{2,1,0:T(8,128)}, u32[]{:S(2)}) copy-start(s32[1,8,128]{2,1,0:T(8,128)} %param.11) | copy-start | bytes 12292
  9.5 10.7 %collective-permute-start.4 = (f32[28,8,128]{2,1,0:T(8,128)S(1)}, f32[28,8,128]{2,1,0:T(8,128)S(1)}, u32[]{:S(2)}, u32[]{:S(2)}) collective-permute-start(f32[28,8,128]{2,1,0:T(8,128)S(1)} %pad_maximum_fusion.q_ref), channel_id=1, source_target_pairs={{0,28},{1,29},{2,30},{3,31},{4,0},{5,1},{6,2},{7,3},{8,4},{9,5},{1... | collective-permute-start | bytes 344072 | tf_op jit(solution)/shard_map/ppermute | solution.py:959
  14.1 7.9 %collective-permute-start.3 = (f32[28,8,128]{2,1,0:T(8,128)S(1)}, f32[28,8,128]{2,1,0:T(8,128)S(1)}, u32[]{:S(2)}, u32[]{:S(2)}) collective-permute-start(f32[28,8,128]{2,1,0:T(8,128)S(1)} %pad_maximum_fusion.q_ref), channel_id=1, source_target_pairs={{0,4},{1,5},{2,6},{3,7},{4,8},{5,9},{6,10},{7,11},{8,12},{9,13},{1... | collective-permute-start | bytes 344072 | tf_op jit(solution)/shard_map/ppermute | solution.py:959
  14.1 6.0 %collective-permute-start.5 = (f32[14,8,128]{2,1,0:T(8,128)S(1)}, f32[14,8,128]{2,1,0:T(8,128)S(1)}, u32[]{:S(2)}, u32[]{:S(2)}) collective-permute-start(f32[14,8,128]{2,1,0:T(8,128)S(1)} %pad_maximum_fusion.1), channel_id=1, source_target_pairs={{0,8},{1,9},{2,26},{3,27},{4,12},{5,13},{6,30},{7,31},{8,16},{9,17... | collective-permute-start | bytes 172040 | tf_op jit(solution)/shard_map/ppermute | solution.py:959
